TPU v7x, 256 devices: a whole 4x4x8 slice. The times are simulated.
256 devices in a mesh: dp: 8 (over y, core), tm: 32 (over z, x).
Axes of the slice: x: 4, y: 4, z: 8, core: 2. Of those that a mesh axis runs over, the one named last changes fastest.
Arguments:
- frames: bfloat16 [65536, 1536], P(('dp', 'tm')), may hold values from -28 to 28, as said below
- seg: int32 [8, 8192], P('dp'), may hold values from 0 to 3, never falling along the last dimension, each value on 1 to 4096 neighbouring positions
- look_back: int32 [8, 32], P('dp'), may hold values 0 or 1
- w_dw: float32 [5, 1536], replicated, may hold values from -2.5 to 2.5
- w_qkv: bfloat16 [1536, 4608], P(None, 'dp'), may hold values from -0.15625 to 0.15625
- w_o: bfloat16 [1536, 1536], replicated, may hold values from -1.5 to 1.5
- cotangent: bfloat16 [65536, 1536], P(('dp', 'tm')), may hold values from -1 to 1
Outputs:
- mixed: bfloat16 [65536, 1536], P(('dp', 'tm'))
- weight_grad: float32 [1536, 1536], P('tm', 'dp')
Inputs may be any that keep to these rules, and one draw needn't show every extreme that they name: Float features; a few short runs of frames may be several times larger than the rest. `seg`: recording numbers never fall along a replica's frames; each recording has 1 to 4096 frames, one exactly 4096.
All inputs are finite; a program needn't handle non-finite values. No bound on the sum of `look_back` on one device may be relied on, other than what follows from the above.
Results may differ from a plain program's by a relative error of at most 0.012.
The roundings to bfloat16 on the way count: a program that leaves them out, or rounds other values in their place, can miss the bound.
Values may be sent and summed in bfloat16 or wider, within the bound.
A program may use at most 128 MiB of HBM per device.

v0:
```python
import math
import jax
import jax.numpy as jnp
from jax import lax
from jax.sharding import PartitionSpec as P

KER = 5
STRETCH = 256


def extended(block, sides, width):
    for axis, dim in sides:
        count = lax.axis_size(axis)
        forward = [(i, i + 1) for i in range(count - 1)]
        backward = [(target, source) for source, target in forward]
        low = lax.ppermute(
            lax.slice_in_dim(block, block.shape[dim] - width, None, axis=dim), axis, forward
        )
        high = lax.ppermute(lax.slice_in_dim(block, 0, width, axis=dim), axis, backward)
        block = jnp.concatenate([low, block, high], axis=dim)
    return block


def swapped(block, axis, distance):
    count = lax.axis_size(axis)
    route = []
    for low in range(count):
        high = low | 1 << distance
        if high != low and high < count:
            route += [(low, high), (high, low)]
    return lax.ppermute(block, axis, route)


def stretch_attention(queries, keys, values, seg_row, look_row, stretch):
    frame_count, heads_here, head_dim = queries.shape
    value_dim = values.shape[2]
    blocks = frame_count // stretch
    query_blocks = queries.reshape(blocks, stretch, heads_here, head_dim)
    key_blocks = keys.reshape(blocks, stretch, heads_here, head_dim)
    value_blocks = values.reshape(blocks, stretch, heads_here, value_dim)
    key_pairs = jnp.concatenate(
        [jnp.concatenate([jnp.zeros_like(key_blocks[:1]), key_blocks[:-1]], 0), key_blocks], 1
    )
    value_pairs = jnp.concatenate(
        [jnp.concatenate([jnp.zeros_like(value_blocks[:1]), value_blocks[:-1]], 0), value_blocks], 1
    )
    seg_blocks = seg_row.reshape(blocks, stretch)
    seg_pairs = jnp.concatenate(
        [jnp.concatenate([jnp.full((1, stretch), -1, jnp.int32), seg_blocks[:-1]], 0), seg_blocks],
        1,
    )
    allow_prev = look_row == 1
    per_step = math.gcd(blocks, max(1, 512 // stretch))
    current = jnp.arange(2 * stretch) >= stretch
    scale = 1.0 / math.sqrt(head_dim)

    def block_step(block_index):
        start = block_index * per_step

        def pick_rows(array):
            return lax.dynamic_slice_in_dim(array, start, per_step, 0)

        scores = (
            jnp.einsum(
                "gqhd,gkhd->ghqk",
                pick_rows(query_blocks),
                pick_rows(key_pairs),
                preferred_element_type=jnp.float32,
            )
            * scale
        )
        same_rec = pick_rows(seg_pairs)[:, None, :] == pick_rows(seg_blocks)[:, :, None]
        allowed = same_rec & (current[None, None, :] | pick_rows(allow_prev)[:, None, None])
        scores = jnp.where(allowed[:, None], scores, -1e30)
        row_max = jnp.max(scores, axis=-1, keepdims=True)
        raw_weights = jnp.exp(scores - row_max)
        probs = (raw_weights / jnp.sum(raw_weights, axis=-1, keepdims=True)).astype(jnp.bfloat16)
        outputs = jnp.einsum(
            "ghqk,gkhv->gqhv", probs, pick_rows(value_pairs), preferred_element_type=jnp.float32
        )
        return outputs.astype(jnp.bfloat16).reshape(per_step * stretch, heads_here * value_dim)

    mixed = lax.map(block_step, jnp.arange(blocks // per_step, dtype=jnp.int32))
    return mixed.reshape(frame_count, heads_here * value_dim)


def local(frames, seg, look_back, w_dw, w_qkv, w_o, cotangent):
    rows = frames.shape[0]
    width = frames.shape[1]
    tm_count = lax.axis_size("tm")
    piece = width // tm_count
    half = KER // 2
    padded = extended(frames, (("tm", 0),), half)
    seg_row = seg[0]
    look_row = look_back[0]
    seg_padded = jnp.pad(seg_row, (half, half), constant_values=-1)
    local_seg = lax.dynamic_slice_in_dim(
        seg_padded, lax.axis_index("tm") * rows, rows + 2 * half, 0
    )
    own_seg = local_seg[half : half + rows]
    total = jnp.zeros((rows, width), jnp.float32)
    for offset in range(KER):
        same_rec = (local_seg[offset : offset + rows] == own_seg).astype(jnp.float32)
        total = (
            total
            + w_dw[offset] * padded[offset : offset + rows].astype(jnp.float32) * same_rec[:, None]
        )
    activ = jax.nn.silu(total).astype(jnp.bfloat16)
    qkv = jnp.dot(
        activ, lax.all_gather(w_qkv, "dp", axis=1, tiled=True), preferred_element_type=jnp.float32
    ).astype(jnp.bfloat16)
    arranged = qkv.reshape(rows, 3, tm_count, piece)
    arrived = lax.all_to_all(arranged, "tm", split_axis=2, concat_axis=0, tiled=True)
    frame_count = arrived.shape[0]
    lower = lax.axis_index("tm") % 2 == 0
    own_pair = arrived[:, 0:2, 0, :]
    other_pair = swapped(own_pair, "tm", 0)
    joined = jnp.where(
        lower,
        jnp.concatenate([own_pair, other_pair], -1),
        jnp.concatenate([other_pair, own_pair], -1),
    )
    queries = joined[:, 0][:, None, :]
    keys = joined[:, 1][:, None, :]
    values = arrived[:, 2, 0, :][:, None, :]
    attended = stretch_attention(queries, keys, values, seg_row, look_row, STRETCH)
    returned = lax.all_to_all(
        attended.reshape(frame_count, 1, piece), "tm", split_axis=0, concat_axis=1, tiled=True
    )
    attn = returned.reshape(rows, width)
    mixed = jnp.dot(attn, w_o, preferred_element_type=jnp.float32).astype(jnp.bfloat16)
    grad_term = lax.dot_general(
        attn, cotangent, (((0,), (0,)), ((), ())), preferred_element_type=jnp.float32
    )
    row_share = lax.psum_scatter(grad_term, "tm", scatter_dimension=0, tiled=True)
    weight_grad = lax.psum_scatter(row_share, "dp", scatter_dimension=1, tiled=True)
    return (mixed, weight_grad)


def solution(mesh):
    placed = (
        P(("dp", "tm"), None),
        P("dp", None),
        P("dp", None),
        P(),
        P(None, "dp"),
        P(),
        P(("dp", "tm"), None),
    )
    return jax.shard_map(
        local,
        mesh=mesh,
        in_specs=placed,
        out_specs=(P(("dp", "tm"), None), P("tm", "dp")),
        check_vma=False,
    )
```

profile of v0, /device:TPU:4, one launch (start us, length us, event | category | flops | bytes accessed | tf_op | source)
XLA Modules:
  0.0 700.8 jit_solution(11983358287464709644)
XLA Ops:
  8.4 2.4 collective-permute-start.1
  10.9 3.4 collective-permute-start
  14.6 2.0 collective-permute-done
  16.6 72.7 %all-gather.2.cloned.1.call-done = bf16[1536,4608]{0,1:T(8,128)(2,1)} async-done(((bf16[1536,576]{0,1:T(8,128)(2,1)}), bf16[1536,4608]{0,1:T(8,128)(2,1)}) %all-gather.2.cloned.1.call-update) | async-done | bytes 14155792 | tf_op jit(solution)/shard_map/all_gather | solution.py:110
  89.4 11.5 %convolution_convert_fusion.1 = bf16[256,4608]{1,0:T(8,128)(2,1)} fusion(bf16[1536,4608]{0,1:T(8,128)(2,1)} %all-gather.2.cloned.1.call-done, bf16[256,1536]{1,0:T(8,128)(2,1)S(1)} %copy-done.4, bf16[2,1536]{1,0:T(2,128)(2,1)S(1)} %collective-permute-done, bf16[258,1536]{1,0:T(8,128)(2,1)S(1)} %constant_dynamic-update-slice_fusion.1, ...), kind=kOutput, calls=%fused_computation.23 | convolution fusion | flops 3636461568 | bytes 18925568 | tf_op jit(solution)/shard_map/dot_general | solution.py:109
  100.8 2.8 copy.24
  103.8 66.5 %all_to_all.33 = bf16[256,3,32,48]{0,3,1,2:T(8,128)(2,1)S(1)} all-to-all(bf16[256,3,32,48]{0,3,1,2:T(8,128)(2,1)S(1)} %copy.25), channel_id=1, replica_groups=mesh['dp'=8,'tm'=32] {'tm'}, dimensions={2} | all-to-all | bytes 4718592 | tf_op jit(solution)/shard_map/all_to_all | solution.py:113
  170.6 1.3 slice_bitcast_fusion
  171.9 1.3 collective-permute-start.2
  177.0 1.6 fusion.13
  178.6 29.1 %collective-permute-done.2 = bf16[8192,2,48]{0,2,1:T(8,128)(2,1)} collective-permute-done((bf16[8192,2,48]{0,2,1:T(8,128)(2,1)}, bf16[8192,2,48]{0,2,1:T(8,128)(2,1)}, u32[]{:S(2)}, u32[]{:S(2)}) %collective-permute-start.2) | collective-permute-done | bytes 1572896 | tf_op jit(solution)/shard_map/ppermute | solution.py:31
  207.6 3.8 maximum_select_fusion
  211.7 1.3 slice.119
  213.0 1.6 copy.44
  214.6 3.6 slice.109
  218.2 1.6 copy.43
  220.6 2.9 fusion.11
  223.5 98.1 %while.11 = (s32[]{:T(128)}, bf16[16,512,48]{1,2,0:T(8,128)(2,1)S(1)}, s32[16]{0:T(128)S(1)}, bf16[32,512,1,48]{1,0,3,2:T(8,128)(2,1)}, s32[32,512]{1,0:T(8,128)...) while((s32[]{:T(128)}, ...), condition=%wide.region_3.4_spmd.clone, body=%wide.region_0.3_spmd.clone.sunk | while | flops 77621248 | bytes 3646681 | solution.py:83
  224.7 1.3 constant_dynamic-slice_fusion.12
  226.1 1.1 constant_dynamic-slice_fusion.13
  228.0 1.1 constant_dynamic-slice_fusion.14
  230.9 1.3 constant_dynamic-slice_fusion.12
  232.2 1.1 constant_dynamic-slice_fusion.13
  237.0 1.3 constant_dynamic-slice_fusion.12
  238.3 1.1 constant_dynamic-slice_fusion.13
  243.1 1.3 constant_dynamic-slice_fusion.12
  244.5 1.1 constant_dynamic-slice_fusion.13
  249.3 1.3 constant_dynamic-slice_fusion.12
  250.6 1.1 constant_dynamic-slice_fusion.13
  255.4 1.3 constant_dynamic-slice_fusion.12
  256.7 1.1 constant_dynamic-slice_fusion.13
  261.5 1.3 constant_dynamic-slice_fusion.12
  262.9 1.1 constant_dynamic-slice_fusion.13
  267.7 1.3 constant_dynamic-slice_fusion.12
  269.0 1.1 constant_dynamic-slice_fusion.13
  273.8 1.3 constant_dynamic-slice_fusion.12
  275.1 1.1 constant_dynamic-slice_fusion.13
  279.9 1.3 constant_dynamic-slice_fusion.12
  281.3 1.1 constant_dynamic-slice_fusion.13
  286.1 1.3 constant_dynamic-slice_fusion.12
  287.4 1.1 constant_dynamic-slice_fusion.13
  292.2 1.3 constant_dynamic-slice_fusion.12
  293.5 1.1 constant_dynamic-slice_fusion.13
  298.3 1.3 constant_dynamic-slice_fusion.12
  299.7 1.1 constant_dynamic-slice_fusion.13
  304.5 1.3 constant_dynamic-slice_fusion.12
  305.8 1.1 constant_dynamic-slice_fusion.13
  310.6 1.3 constant_dynamic-slice_fusion.12
  311.9 1.1 constant_dynamic-slice_fusion.13
  316.7 1.3 constant_dynamic-slice_fusion.12
  318.1 1.1 constant_dynamic-slice_fusion.13
  322.5 2.0 copy.34
  324.5 6.2 reshape.89
  331.2 45.2 %reduce.20 = bf16[8192,48]{1,0:T(8,128)(2,1)S(1)} reduce(bf16[8192,1,48]{2,1,0:T(2,128)(2,1)} %reshape.89, bf16[]{:T(256)} %broadcast.84), dimensions={1}, to_apply=%reshape.89.reduce_sub_computation | reduce | bytes 1572866 | tf_op jit(solution)/shard_map/reshape;reshape | solution.py:128
  376.4 4.2 reshape.107
  380.6 27.1 %all_to_all.34 = bf16[32,2,6144]{2,1,0:T(2,128)(2,1)S(1)} all-to-all(bf16[32,2,6144]{2,1,0:T(2,128)(2,1)} %reshape.107), channel_id=1, replica_groups=mesh['dp'=8,'tm'=32] {'tm'}, dimensions={0} | all-to-all | bytes 1572864 | tf_op jit(solution)/shard_map/all_to_all | solution.py:127
  407.7 7.9 %reshape.108 = bf16[8192,1,48]{2,1,0:T(2,128)(2,1)} reshape(bf16[32,2,6144]{2,1,0:T(2,128)(2,1)S(1)} %all_to_all.34) | data formatting | bytes 1572864
  415.5 8.1 %copy.32 = bf16[8192,1,48]{0,2,1:T(8,128)(2,1)S(1)} copy(bf16[8192,1,48]{2,1,0:T(2,128)(2,1)} %reshape.108) | data formatting | bytes 1572864 | tf_op jit(solution)/shard_map/all_to_all | solution.py:127
  424.3 5.0 fusion.34
  429.4 227.5 %reduce-scatter.5.cloned.1.call-done = f32[48,1536]{1,0:T(8,128)} async-done(((f32[1536,1536]{1,0:T(8,128)}), f32[48,1536]{1,0:T(8,128)}) %reduce-scatter.5.cloned.1.call-update) | async-done | bytes 294928 | tf_op jit(solution)/shard_map/reduce_scatter | solution.py:135
  656.9 2.1 copy.35
  659.1 4.6 convolution_convert_fusion.2
  663.7 29.0 %reduce-scatter.7.cloned.1.call-done = f32[192,48]{1,0:T(8,128)} async-done(((f32[1536,48]{1,0:T(8,128)}), f32[192,48]{1,0:T(8,128)}) %reduce-scatter.7.cloned.1.call-update) | async-done | bytes 36880
  692.7 1.6 copy.36
  (243 shorter events, 54.9 us)
Async XLA Ops:
  7.2 417.1 %copy-start = (bf16[256,1536]{1,0:T(8,128)(2,1)S(1)}, bf16[256,1536]{1,0:T(8,128)(2,1)}, u32[]{:S(2)}) copy-start(bf16[256,1536]{1,0:T(8,128)(2,1)} %param.15) | copy-start | bytes 2359300
  7.2 1.2 copy-start.4
  7.2 7.1 %copy-start.7 = (s32[1,8192]{1,0:T(1,128)S(1)}, s32[1,8192]{1,0:T(1,128)}, u32[]{:S(2)}) copy-start(s32[1,8192]{1,0:T(1,128)} %param.10) | copy-start | bytes 98308
  7.2 7.3 %copy-start.8 = (f32[5,1536]{1,0:T(8,128)S(1)}, f32[5,1536]{1,0:T(8,128)}, u32[]{:S(2)}) copy-start(f32[5,1536]{1,0:T(8,128)} %param.12) | copy-start | bytes 92164
  7.2 82.2 %all-gather.2.cloned.1.call-start = ((), (), s32[]{:S(2)}) async-start(), calls=%async_computation.4 | async-start | bytes 15925248 | tf_op jit(solution)/shard_map/all_gather | solution.py:110
  7.9 649.0 %reduce-scatter.5.cloned.1.call-start = ((), (), s32[]{:S(2)}) async-start(), calls=%async_computation.5 | async-start | bytes 9732096 | tf_op jit(solution)/shard_map/reduce_scatter | solution.py:135
  8.4 6.2 collective-permute-start.1
  10.9 5.8 collective-permute-start
  170.6 3.8 copy-start.9
  171.9 35.8 %collective-permute-start.2 = (bf16[8192,2,48]{0,2,1:T(8,128)(2,1)}, bf16[8192,2,48]{0,2,1:T(8,128)(2,1)}, u32[]{:S(2)}, u32[]{:S(2)}) collective-permute-start(bf16[8192,2,48]{0,2,1:T(8,128)(2,1)} %slice_bitcast_fusion), channel_id=1, source_target_pairs={{0,1},{1,0},{2,3},{3,2},{4,5},{5,4},{6,7},{7,6},{8,9},{9,8},{10,11... | collective-permute-start | bytes 4718600 | tf_op jit(solution)/shard_map/ppermute | solution.py:31
  175.4 1.1 copy-start.3
  218.2 1.6 copy-start.1
  218.2 2.4 copy-start.2
  220.6 2.9 copy-start.5
  321.6 0.9 copy-start.6
  429.3 263.3 %reduce-scatter.7.cloned.1.call-start = ((), (), s32[]{:S(2)}) async-start(), calls=%async_computation.6 | async-start | bytes 884736
Sparse Core Ops, SparseCore 0:
  9.9 79.4 all-gather.1
  429.5 227.4 reduce-scatter.4
  659.5 33.1 reduce-scatter.6
where the time goes:
time: 704 us; the launch traced here: 701 us
  waiting for transfers between devices  361 us (51%)
  local copies, waits for them, and re-layouts  121 us (17%)
  blocking collectives  93.6 us (13%)
  other arithmetic  55.5 us (8%)
  matrix products  36.9 us (5%)
  between operations  14 us (2%)
  loops' own time  11.7 us (2%)
  starting transfers between devices  7.23 us (1%)
    reduce_scatter x1, waiting for transfers between devices, local(): lax.psum_scatter(grad_term, 'tm', scatter_dimension=0, tiled=True)  228 us
    all_gather x1, waiting for transfers between devices, local(): lax.all_gather(w_qkv, 'dp', axis=1, tiled=True)  72.7 us
    all_to_all x1, blocking collectives, local(): lax.all_to_all(arranged, 'tm', split_axis=2, concat_axis=0, tiled=True)  66.5 us
    dynamic_slice x96, local copies, waits for them, and re-layouts, pick_rows(): return lax.dynamic_slice_in_dim(array, start, per_step, 0)  58.5 us
    another operation x1, other arithmetic, local(): attended.reshape(frame_count, 1, piece)  45.2 us
    unnamed x4, waiting for transfers between devices  29.7 us
    ppermute x1, waiting for transfers between devices, swapped(): return lax.ppermute(block, axis, route)  29.1 us
    all_to_all x1, blocking collectives, local(): lax.all_to_all(attended.reshape(frame_count, 1, piece), 'tm', split_axis=...  27.1 us
  transfers between devices with their start and end apart: 6, of which 5 were waited for; matrix products, arithmetic and copies ran while one was open for 1% of the time, Pallas kernels for 0%

commit v1 on v0

--- a/solution.py
+++ b/solution.py
@@ -106,9 +106,12 @@
             + w_dw[offset] * padded[offset : offset + rows].astype(jnp.float32) * same_rec[:, None]
         )
     activ = jax.nn.silu(total).astype(jnp.bfloat16)
-    qkv = jnp.dot(
-        activ, lax.all_gather(w_qkv, "dp", axis=1, tiled=True), preferred_element_type=jnp.float32
-    ).astype(jnp.bfloat16)
+    _draft_strings = lambda array_here: jnp.concatenate(
+        jax.lax.all_to_all(jnp.stack([array_here] * jax.lax.axis_size("dp")), "dp", 0, 0), axis=1
+    )
+    qkv = jnp.dot(activ, _draft_strings(w_qkv), preferred_element_type=jnp.float32).astype(
+        jnp.bfloat16
+    )
     arranged = qkv.reshape(rows, 3, tm_count, piece)
     arrived = lax.all_to_all(arranged, "tm", split_axis=2, concat_axis=0, tiled=True)
     frame_count = arrived.shape[0]

time: 704 us -> 789 us (1.12)
  waiting for transfers between devices: 361 us -> 432 us
    all_to_all x0 -> x1, waiting for transfers between devices: none -> 148 us  [local(): jax.lax.all_to_all(jnp.stack([array_here] * jax.lax.axis_size('dp')), 'dp...]
    all_gather x1 -> x0, waiting for transfers between devices: 72.7 us -> none  [local(): lax.all_gather(w_qkv, 'dp', axis=1, tiled=True)]
    unnamed x30 -> x28, local copies, waits for them, and re-layouts: 22.9 us -> 20.6 us
    unnamed x4 -> x3, waiting for transfers between devices: 29.7 us -> 29.2 us
where the time goes in v1:
time: 789 us; the launch traced here: 786 us
  waiting for transfers between devices  432 us (55%)
  local copies, waits for them, and re-layouts  128 us (16%)
  blocking collectives  94.7 us (12%)
  other arithmetic  55.5 us (7%)
  matrix products  36.8 us (5%)
  between operations  14.4 us (2%)
  starting transfers between devices  12.8 us (2%)
  loops' own time  11.9 us (2%)
    reduce_scatter x1, waiting for transfers between devices, local(): lax.psum_scatter(grad_term, 'tm', scatter_dimension=0, tiled=True)  227 us
    all_to_all x1, waiting for transfers between devices, local(): jax.lax.all_to_all(jnp.stack([array_here] * jax.lax.axis_size('dp')), 'dp...  148 us
    all_to_all x1, blocking collectives, local(): lax.all_to_all(arranged, 'tm', split_axis=2, concat_axis=0, tiled=True)  67.4 us
    dynamic_slice x96, local copies, waits for them, and re-layouts, pick_rows(): return lax.dynamic_slice_in_dim(array, start, per_step, 0)  58.5 us
    another operation x1, other arithmetic, local(): attended.reshape(frame_count, 1, piece)  45.2 us
    unnamed x3, waiting for transfers between devices  29.2 us
    all_to_all x1, blocking collectives, local(): lax.all_to_all(attended.reshape(frame_count, 1, piece), 'tm', split_axis=...  27.4 us
    ppermute x1, waiting for transfers between devices, swapped(): return lax.ppermute(block, axis, route)  26.6 us
  transfers between devices with their start and end apart: 6, of which 5 were waited for; matrix products, arithmetic and copies ran while one was open for 1% of the time, Pallas kernels for 0%

profile of v1, /device:TPU:4, one launch (start us, length us, event | category | flops | bytes accessed | tf_op | source)
XLA Modules:
  0.0 786.1 jit_solution(8862140214266733995)
XLA Ops:
  7.2 7.2 stack.2
  14.4 5.6 all-to-all-start
  20.1 3.1 collective-permute-start
  23.2 2.7 collective-permute-start.1
  26.3 2.4 collective-permute-done.1
  28.7 147.7 %all-to-all-done = bf16[8,1536,576]{1,2,0:T(8,128)(2,1)} async-done(((bf16[8,1536,576]{1,2,0:T(8,128)(2,1)}), bf16[8,1536,576]{1,2,0:T(8,128)(2,1)}, u32[]{:S(2)}, u32[]{:S(2)}) %all-to-all-start) | async-done | bytes 14155808 | tf_op jit(solution)/shard_map/all_to_all | solution.py:110
  176.4 11.5 %convolution_convert_fusion.1 = bf16[256,4608]{1,0:T(8,128)(2,1)} fusion(bf16[1536,4608]{0,1:T(8,128)(2,1)} %bitcast.2, bf16[256,1536]{1,0:T(8,128)(2,1)S(1)} %copy-done.3, bf16[2,1536]{1,0:T(2,128)(2,1)S(1)} %collective-permute-done, bf16[258,1536]{1,0:T(8,128)(2,1)S(1)} %constant_dynamic-update-slice_fusion.1, f32[256]{0:T(256)S(1)} %get-tuple-element.134, ...), kind=kOutput, calls=%fused_computation.23 | convolution fusion | flops 3636461568 | bytes 18925568 | tf_op jit(solution)/shard_map/dot_general | solution.py:112
  187.8 2.8 copy.25
  190.8 67.4 %all_to_all.38 = bf16[256,3,32,48]{0,3,1,2:T(8,128)(2,1)S(1)} all-to-all(bf16[256,3,32,48]{0,3,1,2:T(8,128)(2,1)S(1)} %copy.26), channel_id=1, replica_groups=mesh['dp'=8,'tm'=32] {'tm'}, dimensions={2} | all-to-all | bytes 4718592 | tf_op jit(solution)/shard_map/all_to_all | solution.py:116
  258.5 1.3 slice_bitcast_fusion
  259.7 1.2 collective-permute-start.2
  264.1 1.7 slice.102
  266.0 1.6 fusion.13
  267.6 26.6 %collective-permute-done.2 = bf16[8192,2,48]{0,2,1:T(8,128)(2,1)} collective-permute-done((bf16[8192,2,48]{0,2,1:T(8,128)(2,1)}, bf16[8192,2,48]{0,2,1:T(8,128)(2,1)}, u32[]{:S(2)}, u32[]{:S(2)}) %collective-permute-start.2) | collective-permute-done | bytes 1572896 | tf_op jit(solution)/shard_map/ppermute | solution.py:31
  294.1 3.8 maximum_select_fusion
  298.2 1.2 slice.119
  299.5 1.6 copy.44
  301.1 3.6 slice.109
  306.1 2.9 fusion.11
  309.0 98.2 %while.11 = (s32[]{:T(128)}, bf16[16,512,48]{1,2,0:T(8,128)(2,1)S(1)}, s32[16]{0:T(128)S(1)}, bf16[32,512,1,48]{1,0,3,2:T(8,128)(2,1)}, s32[32,512]{1,0:T(8,128)...) while((s32[]{:T(128)}, ...), condition=%wide.region_3.4_spmd.clone, body=%wide.region_0.3_spmd.clone.sunk | while | flops 77621248 | bytes 3646689 | solution.py:83
  310.4 1.3 constant_dynamic-slice_fusion.12
  311.7 1.1 constant_dynamic-slice_fusion.13
  316.5 1.3 constant_dynamic-slice_fusion.12
  317.9 1.1 constant_dynamic-slice_fusion.13
  322.7 1.3 constant_dynamic-slice_fusion.12
  324.0 1.1 constant_dynamic-slice_fusion.13
  328.8 1.3 constant_dynamic-slice_fusion.12
  330.2 1.1 constant_dynamic-slice_fusion.13
  335.0 1.3 constant_dynamic-slice_fusion.12
  336.3 1.1 constant_dynamic-slice_fusion.13
  341.1 1.3 constant_dynamic-slice_fusion.12
  342.4 1.1 constant_dynamic-slice_fusion.13
  347.2 1.3 constant_dynamic-slice_fusion.12
  348.6 1.1 constant_dynamic-slice_fusion.13
  353.4 1.3 constant_dynamic-slice_fusion.12
  354.7 1.1 constant_dynamic-slice_fusion.13
  359.5 1.3 constant_dynamic-slice_fusion.12
  360.9 1.1 constant_dynamic-slice_fusion.13
  365.7 1.3 constant_dynamic-slice_fusion.12
  367.0 1.1 constant_dynamic-slice_fusion.13
  371.8 1.3 constant_dynamic-slice_fusion.12
  373.1 1.1 constant_dynamic-slice_fusion.13
  377.9 1.3 constant_dynamic-slice_fusion.12
  379.3 1.1 constant_dynamic-slice_fusion.13
  384.1 1.3 constant_dynamic-slice_fusion.12
  385.4 1.1 constant_dynamic-slice_fusion.13
  390.2 1.3 constant_dynamic-slice_fusion.12
  391.6 1.1 constant_dynamic-slice_fusion.13
  396.3 1.3 constant_dynamic-slice_fusion.12
  397.7 1.1 constant_dynamic-slice_fusion.13
  402.5 1.3 constant_dynamic-slice_fusion.12
  408.1 2.0 copy.35
  410.0 6.2 reshape.99
  416.7 45.2 %reduce.20 = bf16[8192,48]{1,0:T(8,128)(2,1)S(1)} reduce(bf16[8192,1,48]{2,1,0:T(2,128)(2,1)} %reshape.99, bf16[]{:T(256)} %broadcast.86), dimensions={1}, to_apply=%reshape.99.reduce_sub_computation | reduce | bytes 1572866 | tf_op jit(solution)/shard_map/reshape;reshape | solution.py:131
  462.0 4.2 reshape.117
  466.2 27.4 %all_to_all.39 = bf16[32,2,6144]{2,1,0:T(2,128)(2,1)S(1)} all-to-all(bf16[32,2,6144]{2,1,0:T(2,128)(2,1)} %reshape.117), channel_id=1, replica_groups=mesh['dp'=8,'tm'=32] {'tm'}, dimensions={0} | all-to-all | bytes 1572864 | tf_op jit(solution)/shard_map/all_to_all | solution.py:130
  493.6 7.9 %reshape.118 = bf16[8192,1,48]{2,1,0:T(2,128)(2,1)} reshape(bf16[32,2,6144]{2,1,0:T(2,128)(2,1)S(1)} %all_to_all.39) | data formatting | bytes 1572864
  501.4 8.1 %copy.33 = bf16[8192,1,48]{0,2,1:T(8,128)(2,1)S(1)} copy(bf16[8192,1,48]{2,1,0:T(2,128)(2,1)} %reshape.118) | data formatting | bytes 1572864 | tf_op jit(solution)/shard_map/all_to_all | solution.py:130
  510.2 5.0 fusion.34
  515.3 226.5 %reduce-scatter.5.cloned.1.call-done = f32[48,1536]{1,0:T(8,128)} async-done(((f32[1536,1536]{1,0:T(8,128)}), f32[48,1536]{1,0:T(8,128)}) %reduce-scatter.5.cloned.1.call-update) | async-done | bytes 294928 | tf_op jit(solution)/shard_map/reduce_scatter | solution.py:138
  741.8 2.1 copy.36
  743.9 4.6 convolution_convert_fusion.2
  748.6 29.1 %reduce-scatter.7.cloned.1.call-done = f32[192,48]{1,0:T(8,128)} async-done(((f32[1536,48]{1,0:T(8,128)}), f32[192,48]{1,0:T(8,128)}) %reduce-scatter.7.cloned.1.call-update) | async-done | bytes 36880
  777.7 1.6 copy.37
  (241 shorter events, 56.1 us)
Async XLA Ops:
  7.2 503.0 %copy-start = (bf16[256,1536]{1,0:T(8,128)(2,1)S(1)}, bf16[256,1536]{1,0:T(8,128)(2,1)}, u32[]{:S(2)}) copy-start(bf16[256,1536]{1,0:T(8,128)(2,1)} %param.15) | copy-start | bytes 2359300
  14.3 5.7 copy-start.3
  14.3 11.6 %copy-start.6 = (s32[1,8192]{1,0:T(1,128)S(1)}, s32[1,8192]{1,0:T(1,128)}, u32[]{:S(2)}) copy-start(s32[1,8192]{1,0:T(1,128)} %param.10) | copy-start | bytes 98308
  14.4 162.0 %all-to-all-start = ((bf16[8,1536,576]{1,2,0:T(8,128)(2,1)}), bf16[8,1536,576]{1,2,0:T(8,128)(2,1)}, u32[]{:S(2)}, u32[]{:S(2)}) async-start(bf16[8,1536,576]{1,2,0:T(8,128)(2,1)} %stack.2), calls=%async_computation | async-start | bytes 28311552 | tf_op jit(solution)/shard_map/all_to_all | solution.py:110
  20.0 6.2 copy-start.7
  20.0 721.8 %reduce-scatter.5.cloned.1.call-start = ((), (), s32[]{:S(2)}) async-start(), calls=%async_computation.5 | async-start | bytes 9732096 | tf_op jit(solution)/shard_map/reduce_scatter | solution.py:138
  20.1 8.7 %collective-permute-start = (bf16[2,1536]{1,0:T(2,128)(2,1)S(1)}, bf16[2,1536]{1,0:T(2,128)(2,1)S(1)}, u32[]{:S(2)}, u32[]{:S(2)}) collective-permute-start(bf16[2,1536]{1,0:T(2,128)(2,1)S(1)} %get-tuple-element.130), channel_id=1, source_target_pairs={{0,1},{1,2},{2,3},{3,4},{4,5},{5,6},{6,7},{7,8},{8,9},{9,10},{10,1... | collective-permute-start | bytes 18440 | tf_op jit(solution)/shard_map/ppermute | solution.py:16
  23.2 5.5 collective-permute-start.1
  258.4 3.7 copy-start.8
  259.7 34.4 %collective-permute-start.2 = (bf16[8192,2,48]{0,2,1:T(8,128)(2,1)}, bf16[8192,2,48]{0,2,1:T(8,128)(2,1)}, u32[]{:S(2)}, u32[]{:S(2)}) collective-permute-start(bf16[8192,2,48]{0,2,1:T(8,128)(2,1)} %slice_bitcast_fusion), channel_id=1, source_target_pairs={{0,1},{1,0},{2,3},{3,2},{4,5},{5,4},{6,7},{7,6},{8,9},{9,8},{10,11... | collective-permute-start | bytes 4718600 | tf_op jit(solution)/shard_map/ppermute | solution.py:31
  264.1 1.7 copy-start.2
  304.7 1.4 copy-start.1
  306.1 2.9 copy-start.4
  407.2 0.9 copy-start.5
  515.2 262.5 %reduce-scatter.7.cloned.1.call-start = ((), (), s32[]{:S(2)}) async-start(), calls=%async_computation.6 | async-start | bytes 884736
Sparse Core Ops, SparseCore 0:
  515.3 226.4 reduce-scatter.4
  744.3 33.3 reduce-scatter.6
